TPU v7x, 32 devices: a whole 2x2x4 slice. The times are simulated.
32 devices in a mesh: cfg: 2 (over x), tm: 16 (over z, y, core).
Axes of the slice: x: 2, y: 2, z: 4, core: 2. Of those that a mesh axis runs over, the one named last changes fastest.
Arguments:
- elemental: bfloat16 [32, 1024, 1024], P(('cfg', 'tm')), parts along dimension 0, may hold values from -0.1875 to 0.1875
- peramb: bfloat16 [32, 3, 1024, 1024], P(('cfg', 'tm')), parts along dimension 0, may hold values from -0.1875 to 0.1875
- seps: int32 [16, 3], P('tm'), may hold values from -2 to 2, as said below
Outputs:
- corr: float32 [32, 3], P(('cfg', 'tm')), parts along dimension 0
- pair: float32 [32, 3], P(('cfg', 'tm')), parts along dimension 0
There are 2 independent parts, one for each index of `cfg`. A program takes and returns all parts, laid end to end along the dimension named above; an argument that names none is the same for every part. Nothing has to cross between parts.
Inputs may be any that keep to these rules, and one draw needn't show every extreme that they name: `seps`: every separation is nonzero; source slice 0 has separation 2 as its first pair and source slice 1 has -2.
All inputs are finite; a program needn't handle non-finite values.
Results may differ from a plain program's by a relative error of at most 0.0003.
Values may be sent and summed in bfloat16 or wider, within the bound.
A program may use at most 64 MiB of HBM per device.

v0:
```python
import jax
import jax.numpy as jnp
from jax import lax
from jax.sharding import PartitionSpec as P

NEV = 256
H = 2


def from_behind(x, axis, by):
    peers = lax.axis_size(axis)
    return lax.ppermute(x, axis, [(i, (i + by) % peers) for i in range(peers)])


def body(elemental, peramb, seps):
    own = elemental[0]
    tiles = peramb[0]
    needed_block = seps[0]
    count = tiles.shape[0]
    width = own.shape[0]
    block_rows = jnp.arange(width, dtype=jnp.int32)
    sign = jnp.where(block_rows // NEV < 2, 1.0, -1.0).astype(jnp.float32)
    signs = (sign[:, None] * sign[None, :]).astype(jnp.bfloat16)
    chosen = [jnp.zeros_like(own) for k in range(count)]

    def keep(chosen, offset, received_block):
        return [
            jnp.where(needed_block[k] == offset, received_block, chosen[k]) for k in range(count)
        ]

    current = from_behind(own, "tm", H)
    chosen = keep(chosen, -H, current)
    for offset in range(1 - H, H + 1):
        current = from_behind(current, "tm", -1)
        if offset != 0:
            chosen = keep(chosen, offset, current)
    values = []
    for k in range(count):
        right = lax.dot_general(
            tiles[k] * signs, own, (((1,), (1,)), ((), ())), preferred_element_type=jnp.float32
        )
        left = jnp.dot(chosen[k], tiles[k], preferred_element_type=jnp.float32)
        values.append(jnp.sum(left * right))
    corr = jnp.stack(values)[None, :]
    nearby_device = from_behind(corr, "tm", -1)
    return (corr, corr * nearby_device)


def solution(mesh):
    in_specs = (P(("cfg", "tm"), None, None), P(("cfg", "tm"), None, None, None), P("tm", None))
    out_specs = (P(("cfg", "tm"), None), P(("cfg", "tm"), None))
    return jax.shard_map(body, mesh=mesh, in_specs=in_specs, out_specs=out_specs, check_vma=False)
```

profile of v0, /device:TPU:0, one launch (start us, length us, event | category | flops | bytes accessed | tf_op | source)
XLA Modules:
  0.0 181.3 jit_solution(4168868092468145548)
XLA Ops:
  0.6 3.0 %collective-permute-start = (bf16[1024,1024]{1,0:T(8,128)(2,1)}, bf16[1024,1024]{1,0:T(8,128)(2,1)S(1)}, u32[]{:S(2)}, u32[]{:S(2)}) collective-permute-start(bf16[1024,1024]{1,0:T(8,128)(2,1)} %bitcast.44), channel_id=1, source_target_pairs={{0,2},{1,3},{2,4},{3,5},{4,6},{5,7},{6,8},{7,9},{8,10},{9,11},{10,... | collective-permute-start | bytes 6291464 | tf_op jit(solution)/shard_map/ppermute | solution.py:12
  3.6 48.9 %collective-permute-done = bf16[1024,1024]{1,0:T(8,128)(2,1)S(1)} collective-permute-done((bf16[1024,1024]{1,0:T(8,128)(2,1)}, bf16[1024,1024]{1,0:T(8,128)(2,1)S(1)}, u32[]{:S(2)}, u32[]{:S(2)}) %collective-permute-start) | collective-permute-done | bytes 2097184 | tf_op jit(solution)/shard_map/ppermute | solution.py:12
  52.5 0.3 collective-permute-start.1
  52.8 23.6 %collective-permute-done.1 = bf16[1024,1024]{1,0:T(8,128)(2,1)S(1)} collective-permute-done((bf16[1024,1024]{1,0:T(8,128)(2,1)S(1)}, bf16[1024,1024]{1,0:T(8,128)(2,1)S(1)}, u32[]{:S(2)}, u32[]{:S(2)}) %collective-permute-start.1) | collective-permute-done | bytes 2097184 | tf_op jit(solution)/shard_map/ppermute | solution.py:12
  76.4 4.6 %collective-permute-start.2 = (bf16[1024,1024]{1,0:T(8,128)(2,1)S(1)}, bf16[1024,1024]{1,0:T(8,128)(2,1)S(1)}, u32[]{:S(2)}, u32[]{:S(2)}) collective-permute-start(bf16[1024,1024]{1,0:T(8,128)(2,1)S(1)} %collective-permute-done.1), channel_id=1, source_target_pairs={{0,15},{1,0},{2,1},{3,2},{4,3},{5,4},{6,5},{7,6},{8,7},{9,8},{10,9... | collective-permute-start | bytes 6291464 | tf_op jit(solution)/shard_map/ppermute | solution.py:12
  81.0 23.6 %collective-permute-done.2 = bf16[1024,1024]{1,0:T(8,128)(2,1)S(1)} collective-permute-done((bf16[1024,1024]{1,0:T(8,128)(2,1)S(1)}, bf16[1024,1024]{1,0:T(8,128)(2,1)S(1)}, u32[]{:S(2)}, u32[]{:S(2)}) %collective-permute-start.2) | collective-permute-done | bytes 2097184 | tf_op jit(solution)/shard_map/ppermute | solution.py:12
  104.5 4.6 %collective-permute-start.3 = (bf16[1024,1024]{1,0:T(8,128)(2,1)S(1)}, bf16[1024,1024]{1,0:T(8,128)(2,1)S(1)}, u32[]{:S(2)}, u32[]{:S(2)}) collective-permute-start(bf16[1024,1024]{1,0:T(8,128)(2,1)S(1)} %collective-permute-done.2), channel_id=1, source_target_pairs={{0,15},{1,0},{2,1},{3,2},{4,3},{5,4},{6,5},{7,6},{8,7},{9,8},{10,9... | collective-permute-start | bytes 6291464 | tf_op jit(solution)/shard_map/ppermute | solution.py:12
  109.1 23.6 %collective-permute-done.3 = bf16[1024,1024]{1,0:T(8,128)(2,1)S(1)} collective-permute-done((bf16[1024,1024]{1,0:T(8,128)(2,1)S(1)}, bf16[1024,1024]{1,0:T(8,128)(2,1)S(1)}, u32[]{:S(2)}, u32[]{:S(2)}) %collective-permute-start.3) | collective-permute-done | bytes 2097184 | tf_op jit(solution)/shard_map/ppermute | solution.py:12
  132.7 4.6 %collective-permute-start.4 = (bf16[1024,1024]{1,0:T(8,128)(2,1)S(1)}, bf16[1024,1024]{1,0:T(8,128)(2,1)S(1)}, u32[]{:S(2)}, u32[]{:S(2)}) collective-permute-start(bf16[1024,1024]{1,0:T(8,128)(2,1)S(1)} %collective-permute-done.3), channel_id=1, source_target_pairs={{0,15},{1,0},{2,1},{3,2},{4,3},{5,4},{6,5},{7,6},{8,7},{9,8},{10,9... | collective-permute-start | bytes 6291464 | tf_op jit(solution)/shard_map/ppermute | solution.py:12
  137.3 1.4 fusion.65
  146.6 0.0 copy-start.1
  146.7 0.0 copy-start.2
  146.7 4.8 %fusion.4 = f32[1024,1024]{1,0:T(8,128)S(1)} fusion(f32[1024]{0:T(1024)S(1)} %fusion.58, bf16[1,3,1024,1024]{3,2,1,0:T(8,128)(2,1)} %param.4, bf16[1,1024,1024]{2,1,0:T(8,128)(2,1)} %param.3), kind=kOutput, calls=%fused_computation.8 | convolution fusion | flops 2150629376 | bytes 8396800 | tf_op jit(solution)/shard_map/dot_general | solution.py:39
  151.4 0.0 copy-done.1
  151.4 0.0 copy-done.2
  151.4 2.4 %fusion.7 = f32[1024,1024]{1,0:T(8,128)S(1)} fusion(f32[1024]{0:T(1024)S(1)} %fusion.58, bf16[1,3,1024,1024]{3,2,1,0:T(8,128)(2,1)S(1)} %copy-done.1, bf16[1,1024,1024]{2,1,0:T(8,128)(2,1)S(1)} %copy-done.2), kind=kOutput, calls=%fused_computation.10 | convolution fusion | flops 2150629376 | bytes 8396800 | tf_op jit(solution)/shard_map/dot_general | solution.py:39
  153.8 2.4 %fusion.10 = f32[1024,1024]{1,0:T(8,128)S(1)} fusion(f32[1024]{0:T(1024)S(1)} %fusion.58, bf16[1,3,1024,1024]{3,2,1,0:T(8,128)(2,1)S(1)} %copy-done.1, bf16[1,1024,1024]{2,1,0:T(8,128)(2,1)S(1)} %copy-done.2), kind=kOutput, calls=%fused_computation.12 | convolution fusion | flops 2150629376 | bytes 8396800 | tf_op jit(solution)/shard_map/dot_general | solution.py:39
  156.2 4.6 %collective-permute-done.4 = bf16[1024,1024]{1,0:T(8,128)(2,1)S(1)} collective-permute-done((bf16[1024,1024]{1,0:T(8,128)(2,1)S(1)}, bf16[1024,1024]{1,0:T(8,128)(2,1)S(1)}, u32[]{:S(2)}, u32[]{:S(2)}) %collective-permute-start.4) | collective-permute-done | bytes 2097184 | tf_op jit(solution)/shard_map/ppermute | solution.py:12
  160.9 3.4 %multiply_reduce_fusion.2 = f32[]{:T(128)} fusion(f32[1024,1024]{1,0:T(8,128)S(1)} %fusion.4, bf16[1024,1024]{1,0:T(8,128)(2,1)S(1)} %collective-permute-done.4, bf16[1024,1024]{1,0:T(8,128)(2,1)S(1)} %collective-permute-done.3, bf16[1024,1024]{1,0:T(8,128)(2,1)S(1)} %collective-permute-done.1, bf16[1024,1024]{1,0:T(8,128)(2,1)S(1)} %collective-permute-done, ...), kind=kOutput, calls=%fused_computation.2 | convolution fusion | flops 2153775104 | bytes 14680072 | tf_op jit(solution)/shard_map/dot_general | solution.py:42
  164.3 3.4 %multiply_reduce_fusion.1 = f32[]{:T(128)} fusion(f32[1024,1024]{1,0:T(8,128)S(1)} %fusion.7, bf16[1024,1024]{1,0:T(8,128)(2,1)S(1)} %collective-permute-done.4, bf16[1024,1024]{1,0:T(8,128)(2,1)S(1)} %collective-permute-done.3, bf16[1024,1024]{1,0:T(8,128)(2,1)S(1)} %collective-permute-done.1, bf16[1024,1024]{1,0:T(8,128)(2,1)S(1)} %collective-permute-done, ...), kind=kOutput, calls=%fused_computation.1 | convolution fusion | flops 2153775104 | bytes 14680072 | tf_op jit(solution)/shard_map/dot_general | solution.py:42
  167.7 3.3 %multiply_reduce_fusion = f32[]{:T(128)} fusion(f32[1024,1024]{1,0:T(8,128)S(1)} %fusion.10, bf16[1024,1024]{1,0:T(8,128)(2,1)S(1)} %collective-permute-done.4, bf16[1024,1024]{1,0:T(8,128)(2,1)S(1)} %collective-permute-done.3, bf16[1024,1024]{1,0:T(8,128)(2,1)S(1)} %collective-permute-done.1, bf16[1024,1024]{1,0:T(8,128)(2,1)S(1)} %collective-permute-done, ...), kind=kOutput, calls=%fused_computation | convolution fusion | flops 2153775104 | bytes 14680072 | tf_op jit(solution)/shard_map/dot_general | solution.py:42
  171.0 1.9 %maximum_bitcast_fusion = f32[1,3]{1,0:T(1,128)S(1)} fusion(f32[1]{0:T(128)} %bitcast.21, f32[1]{0:T(128)} %bitcast.14, f32[1]{0:T(128)} %bitcast.7), kind=kLoop, calls=%fused_computation.64 | loop fusion | flops 6 | bytes 24 | tf_op jit(solution)/shard_map/broadcast_in_dim | solution.py:44
  173.0 0.0 copy-start
  173.0 4.6 %collective-permute-start.5 = (f32[1,3]{1,0:T(1,128)S(1)}, f32[1,3]{1,0:T(1,128)S(1)}, u32[]{:S(2)}, u32[]{:S(2)}) collective-permute-start(f32[1,3]{1,0:T(1,128)S(1)} %maximum_bitcast_fusion), channel_id=1, source_target_pairs={{0,15},{1,0},{2,1},{3,2},{4,3},{5,4},{6,5},{7,6},{8,7},{9,8},{10,9... | collective-permute-start | bytes 44 | tf_op jit(solution)/shard_map/ppermute | solution.py:12
  177.6 1.3 collective-permute-done.5
  178.9 2.4 %fusion.66 = f32[1,3]{1,0:T(1,128)} fusion(f32[1,3]{1,0:T(1,128)S(1)} %collective-permute-done.5, f32[1]{0:T(128)} %bitcast.21, f32[1]{0:T(128)} %bitcast.14, f32[1]{0:T(128)} %bitcast.7), kind=kLoop, calls=%fused_computation.72 | loop fusion | flops 9 | bytes 36 | tf_op jit(solution)/shard_map/mul | solution.py:46
  181.3 0.0 copy-done
  (1 shorter events, 0.0 us)
Async XLA Ops:
  0.6 51.9 %collective-permute-start = (bf16[1024,1024]{1,0:T(8,128)(2,1)}, bf16[1024,1024]{1,0:T(8,128)(2,1)S(1)}, u32[]{:S(2)}, u32[]{:S(2)}) collective-permute-start(bf16[1024,1024]{1,0:T(8,128)(2,1)} %bitcast.44), channel_id=1, source_target_pairs={{0,2},{1,3},{2,4},{3,5},{4,6},{5,7},{6,8},{7,9},{8,10},{9,11},{10,... | collective-permute-start | bytes 6291464 | tf_op jit(solution)/shard_map/ppermute | solution.py:12
  52.5 23.9 %collective-permute-start.1 = (bf16[1024,1024]{1,0:T(8,128)(2,1)S(1)}, bf16[1024,1024]{1,0:T(8,128)(2,1)S(1)}, u32[]{:S(2)}, u32[]{:S(2)}) collective-permute-start(bf16[1024,1024]{1,0:T(8,128)(2,1)S(1)} %collective-permute-done), channel_id=1, source_target_pairs={{0,15},{1,0},{2,1},{3,2},{4,3},{5,4},{6,5},{7,6},{8,7},{9,8},{10,9... | collective-permute-start | bytes 6291464 | tf_op jit(solution)/shard_map/ppermute | solution.py:12
  76.4 28.2 %collective-permute-start.2 = (bf16[1024,1024]{1,0:T(8,128)(2,1)S(1)}, bf16[1024,1024]{1,0:T(8,128)(2,1)S(1)}, u32[]{:S(2)}, u32[]{:S(2)}) collective-permute-start(bf16[1024,1024]{1,0:T(8,128)(2,1)S(1)} %collective-permute-done.1), channel_id=1, source_target_pairs={{0,15},{1,0},{2,1},{3,2},{4,3},{5,4},{6,5},{7,6},{8,7},{9,8},{10,9... | collective-permute-start | bytes 6291464 | tf_op jit(solution)/shard_map/ppermute | solution.py:12
  104.5 28.2 %collective-permute-start.3 = (bf16[1024,1024]{1,0:T(8,128)(2,1)S(1)}, bf16[1024,1024]{1,0:T(8,128)(2,1)S(1)}, u32[]{:S(2)}, u32[]{:S(2)}) collective-permute-start(bf16[1024,1024]{1,0:T(8,128)(2,1)S(1)} %collective-permute-done.2), channel_id=1, source_target_pairs={{0,15},{1,0},{2,1},{3,2},{4,3},{5,4},{6,5},{7,6},{8,7},{9,8},{10,9... | collective-permute-start | bytes 6291464 | tf_op jit(solution)/shard_map/ppermute | solution.py:12
  132.7 28.2 %collective-permute-start.4 = (bf16[1024,1024]{1,0:T(8,128)(2,1)S(1)}, bf16[1024,1024]{1,0:T(8,128)(2,1)S(1)}, u32[]{:S(2)}, u32[]{:S(2)}) collective-permute-start(bf16[1024,1024]{1,0:T(8,128)(2,1)S(1)} %collective-permute-done.3), channel_id=1, source_target_pairs={{0,15},{1,0},{2,1},{3,2},{4,3},{5,4},{6,5},{7,6},{8,7},{9,8},{10,9... | collective-permute-start | bytes 6291464 | tf_op jit(solution)/shard_map/ppermute | solution.py:12
  146.6 4.8 %copy-start.1 = (bf16[1,3,1024,1024]{3,2,1,0:T(8,128)(2,1)S(1)}, bf16[1,3,1024,1024]{3,2,1,0:T(8,128)(2,1)}, u32[]{:S(2)}) copy-start(bf16[1,3,1024,1024]{3,2,1,0:T(8,128)(2,1)} %param.4) | copy-start | bytes 18874372
  146.7 4.8 %copy-start.2 = (bf16[1,1024,1024]{2,1,0:T(8,128)(2,1)S(1)}, bf16[1,1024,1024]{2,1,0:T(8,128)(2,1)}, u32[]{:S(2)}) copy-start(bf16[1,1024,1024]{2,1,0:T(8,128)(2,1)} %param.3) | copy-start | bytes 6291460
  173.0 8.4 %copy-start = (f32[1,3]{1,0:T(1,128)}, f32[1,3]{1,0:T(1,128)S(1)}, u32[]{:S(2)}) copy-start(f32[1,3]{1,0:T(1,128)S(1)} %maximum_bitcast_fusion) | copy-start | bytes 40
  173.0 5.9 %collective-permute-start.5 = (f32[1,3]{1,0:T(1,128)S(1)}, f32[1,3]{1,0:T(1,128)S(1)}, u32[]{:S(2)}, u32[]{:S(2)}) collective-permute-start(f32[1,3]{1,0:T(1,128)S(1)} %maximum_bitcast_fusion), channel_id=1, source_target_pairs={{0,15},{1,0},{2,1},{3,2},{4,3},{5,4},{6,5},{7,6},{8,7},{9,8},{10,9... | collective-permute-start | bytes 44 | tf_op jit(solution)/shard_map/ppermute | solution.py:12
where the time goes:
time: 182 us; the launch traced here: 181 us
  waiting for transfers between devices  125 us (69%)
  starting transfers between devices  21.7 us (12%)
  matrix products  19.7 us (11%)
  between operations  8.6 us (5%)
  other arithmetic  4.39 us (2%)
    ppermute x6, waiting for transfers between devices, from_behind(): return lax.ppermute(x, axis, [(i, (i + by) % peers) for i in range(peers)])  125 us
    ppermute x6, starting transfers between devices, from_behind(): return lax.ppermute(x, axis, [(i, (i + by) % peers) for i in range(peers)])  21.7 us
    dot_general x3, matrix products, body(): left = jnp.dot(chosen[k], tiles[k], preferred_element_type=jnp.float32)  10.2 us
    dot_general x3, matrix products, body(): lax.dot_general(tiles[k] * signs, own, (((1,), (1,)), ((), ())), preferre...  9.54 us
  transfers between devices with their start and end apart: 6, of which 6 were waited for; matrix products, arithmetic and copies ran while one was open for 6% of the time, Pallas kernels for 0%

commit v1 on v0

v1 whole, which is shorter than its diff:
```python
import functools

import jax
import jax.numpy as jnp
from jax import lax
from jax.experimental import pallas as pl
from jax.experimental.pallas import tpu as pltpu
from jax.sharding import PartitionSpec as P

NEV = 256
H = 2
CHUNKS = 16
WINDOW = 3
BLOCK = 256
NT = (((1,), (1,)), ((), ()))
MESH = pl.DeviceIdType.MESH


def kernel(
    peers, seps, e_hbm, p_hbm, corr_ref, pair_ref,
    es, p_v, z, buf, acc, mine, near, local_sem, send, recv, small_sem,
):
    count, width = p_v.shape[0], p_v.shape[1]
    chunk = width // CHUNKS
    block = min(BLOCK, width)
    steps = (width // block) * count

    me = lax.axis_index("tm")
    core = me % 2
    row = (me // 2) % 2
    across = me + 2 - 4 * row
    mate = me + 1 - 2 * core
    onward = (me + peers + 4 - 8 * row) % peers
    upstream = (me + peers - 4 + 8 * row) % peers
    before = (me + peers - 1) % peers
    after = (me + 1) % peers

    barrier = pltpu.get_barrier_semaphore()
    for peer in (across, mate, upstream, after):
        pl.semaphore_signal(barrier, inc=1, device_id={"tm": peer}, device_id_type=MESH)

    e_copy = pltpu.make_async_copy(e_hbm.at[0], es, local_sem.at[0])
    e_copy.start()
    p_copies = [
        pltpu.make_async_copy(p_hbm.at[0, k], p_v.at[k], local_sem.at[1 + k]) for k in range(count)
    ]
    for copy in p_copies:
        copy.start()
    pl.semaphore_wait(barrier, 4)

    def rows_of(j):
        return pl.ds(pl.multiple_of(j * chunk, chunk), chunk)

    def remote(src, slot, j, peer):
        return pltpu.make_async_remote_copy(
            src_ref=src.at[rows_of(j)],
            dst_ref=buf.at[slot, rows_of(j)],
            send_sem=send.at[slot, j],
            recv_sem=recv.at[slot, j],
            device_id={"tm": peer},
            device_id_type=MESH,
        )

    def across_copy(j):
        return remote(e_hbm.at[0], 0, j, across)

    def onward_copy(j):
        return remote(buf.at[0], 1, j, onward)

    def share_copy(j):
        return remote(buf.at[(row + core) % 2], 3, j, mate)

    mate_copy = pltpu.make_async_remote_copy(
        src_ref=e_hbm.at[0],
        dst_ref=buf.at[2],
        send_sem=small_sem.at[2],
        recv_sem=small_sem.at[3],
        device_id={"tm": mate},
        device_id_type=MESH,
    )

    for j in range(WINDOW):
        across_copy(j).start()
    mate_copy.start()

    acc[...] = jnp.zeros_like(acc)
    e_copy.wait()
    sign_row = jnp.where(lax.broadcasted_iota(jnp.int32, (1, width), 1) // NEV < 2, 1.0, -1.0)

    def flip(i, carry):
        at = pl.ds(pl.multiple_of(i * 128, 128), 128)
        es[at, :] = es[at, :] * sign_row.astype(jnp.bfloat16)
        return carry

    lax.fori_loop(0, width // 128, flip, 0)
    for copy in p_copies:
        copy.wait()

    def work(s):
        k = s % count
        first = pl.multiple_of((s // count) * block, block)
        at = pl.ds(first, block)
        index = first + lax.broadcasted_iota(jnp.int32, (block, 1), 0)
        sign = jnp.where(index // NEV < 2, 1.0, -1.0)
        g = lax.dot_general(p_v[k, at, :], es[...], NT, preferred_element_type=jnp.float32) * sign
        high = g.astype(jnp.bfloat16)
        low = (g - high.astype(jnp.float32)).astype(jnp.bfloat16)
        both = jnp.concatenate([high, low], axis=0)
        out = lax.dot_general(both, p_v[k], NT, preferred_element_type=jnp.float32)
        z[k, at, :] = out[:block] + out[block:]

    far = 2 * jnp.int32(1)
    offsets = (far - 2 * far * row, 2 * far * row - far, 1 - 2 * core, 2 * core - 1)

    def contract(slot, j):
        def part(i, totals):
            at = pl.ds(pl.multiple_of(j * chunk + i * 16, 16), 16)
            x = buf[slot, at, :].astype(jnp.float32)
            new = []
            for k in range(count):
                prod = x * z[k, at, :]
                new.append(totals[k] + (prod[:8] + prod[8:]))
            return tuple(new)

        zero = jnp.zeros((8, width), jnp.float32)
        totals = lax.fori_loop(0, chunk // 16, part, (zero,) * count, unroll=True)
        for k in range(count):
            acc[k] += jnp.where(seps[0, k] == offsets[slot], totals[k], 0.0)

    def step(j, carry):
        @pl.when(j < steps)
        def _():
            work(j)

        across_copy(j).wait_recv()
        onward_copy(j).start()
        across_copy(j).wait_send()

        @pl.when(j + WINDOW < CHUNKS)
        def _():
            across_copy(j + WINDOW).start()

        @pl.when(j >= 1)
        def _():
            onward_copy(j - 1).wait_recv()
            share_copy(j - 1).start()

        @pl.when(j == 2)
        def _():
            mate_copy.wait_recv()

        @pl.when(j >= 2)
        def _():
            contract(0, j - 2)
            contract(1, j - 2)
            contract(2, j - 2)
            share_copy(j - 2).wait_recv()
            contract(3, j - 2)

        return carry

    lax.fori_loop(0, CHUNKS, step, 0)
    last = CHUNKS - 1
    for slot in range(3):
        contract(slot, last - 1)
    contract(0, last)
    contract(2, last)
    share_copy(last - 1).wait_recv()
    contract(3, last - 1)
    onward_copy(last).wait_recv()
    share_copy(last).start()
    contract(1, last)
    share_copy(last).wait_recv()
    contract(3, last)

    lane = lax.broadcasted_iota(jnp.int32, (8, 128), 1)
    values = jnp.zeros((8, 128), jnp.float32)
    for k in range(count):
        values = jnp.where(lane == k, jnp.sum(acc[k]), values)
    mine[...] = values
    pass_on = pltpu.make_async_remote_copy(
        src_ref=mine,
        dst_ref=near,
        send_sem=small_sem.at[0],
        recv_sem=small_sem.at[1],
        device_id={"tm": before},
        device_id_type=MESH,
    )
    pass_on.start()

    def drain(j, carry):
        onward_copy(j).wait_send()
        share_copy(j).wait_send()
        return carry

    lax.fori_loop(0, CHUNKS, drain, 0)
    mate_copy.wait_send()
    corr_ref[...] = values[:1, :count]
    pass_on.wait()
    pair_ref[...] = values[:1, :count] * near[:1, :count]


def body(elemental, peramb, seps):
    peers = lax.axis_size("tm")
    count, width = peramb.shape[1], peramb.shape[2]
    small = jax.ShapeDtypeStruct((1, count), jnp.float32)
    return pl.pallas_call(
        functools.partial(kernel, peers),
        out_shape=(small, small),
        in_specs=[
            pl.BlockSpec(memory_space=pltpu.SMEM),
            pl.BlockSpec(memory_space=pl.ANY),
            pl.BlockSpec(memory_space=pl.ANY),
        ],
        out_specs=(pl.BlockSpec(memory_space=pltpu.VMEM),) * 2,
        scratch_shapes=[
            pltpu.VMEM((width, width), jnp.bfloat16),
            pltpu.VMEM((count, width, width), jnp.bfloat16),
            pltpu.VMEM((count, width, width), jnp.float32),
            pltpu.VMEM((4, width, width), jnp.bfloat16),
            pltpu.VMEM((count, 8, width), jnp.float32),
            pltpu.VMEM((8, 128), jnp.float32),
            pltpu.VMEM((8, 128), jnp.float32),
            pltpu.SemaphoreType.DMA((1 + count,)),
            pltpu.SemaphoreType.DMA((4, CHUNKS)),
            pltpu.SemaphoreType.DMA((4, CHUNKS)),
            pltpu.SemaphoreType.DMA((4,)),
        ],
        compiler_params=pltpu.CompilerParams(
            collective_id=0, has_side_effects=True, vmem_limit_bytes=60 * 1024 * 1024
        ),
        cost_estimate=pl.CostEstimate(
            flops=6 * count * width**3, bytes_accessed=2 * (1 + count) * width**2, transcendentals=0
        ),
        name="correlators",
    )(seps, elemental, peramb)


def solution(mesh):
    in_specs = (P(("cfg", "tm"), None, None), P(("cfg", "tm"), None, None, None), P("tm", None))
    out_specs = (P(("cfg", "tm"), None), P(("cfg", "tm"), None))
    return jax.shard_map(body, mesh=mesh, in_specs=in_specs, out_specs=out_specs, check_vma=False)
```

time: 182 us -> 74.2 us (0.41)
  waiting for transfers between devices: 125 us -> 0 us
  Pallas kernels: 0 us -> 71.1 us
  starting transfers between devices: 21.7 us -> 0 us
  matrix products: 19.7 us -> 0 us
  between operations: 8.6 us -> 0.64 us
  other arithmetic: 4.39 us -> 0 us
    ppermute x6 -> x0, waiting for transfers between devices: 125 us -> none  [from_behind(): return lax.ppermute(x, axis, [(i, (i + by) % peers) for i in range(peers)])]
    pallas_call x0 -> x1, Pallas kernels: none -> 71.1 us  [body(): pl.pallas_call(functools.partial(kernel, peers), out_shape=(small, small)...]
    ppermute x6 -> x0, starting transfers between devices: 21.7 us -> none  [from_behind(): return lax.ppermute(x, axis, [(i, (i + by) % peers) for i in range(peers)])]
    dot_general x6 -> x0, matrix products: 19.7 us -> none  [the longest x3 10.2 us: body(): left = jnp.dot(chosen[k], tiles[k], preferred_element_type=jnp.float32)]
    mul x1 -> x0, other arithmetic: 2.45 us -> none  [body(): return (corr, corr * nearby_device)]
    unnamed x6 -> x2, local copies, waits for them, and re-layouts: 0.02 us -> 2.25 us
    broadcast_in_dim x1 -> x0, other arithmetic: 1.94 us -> none  [body(): corr = jnp.stack(values)[None, :]]
  transfers between devices with their start and end apart: 6 -> 0, of which waited for: 6 -> 0; matrix products, arithmetic and copies ran while one was open for 6% -> 0% of each run, Pallas kernels for 0% -> 0%
where the time goes in v1:
time: 74.2 us; the launch traced here: 74 us
  Pallas kernels  71.1 us (96%)
  local copies, waits for them, and re-layouts  2.25 us (3%)
    pallas_call x1, Pallas kernels, body(): pl.pallas_call(functools.partial(kernel, peers), out_shape=(small, small)...  71.1 us
    unnamed x2, local copies, waits for them, and re-layouts  2.25 us

profile of v1, /device:TPU:0, one launch (start us, length us, event | category | flops | bytes accessed | tf_op | source)
XLA Modules:
  0.0 74.0 jit_solution(1178804740870433823)
XLA Ops:
  0.6 71.1 %correlators.1 = (f32[1,3]{1,0:T(1,128)}, f32[1,3]{1,0:T(1,128)}) custom-call(s32[1,3]{1,0:T(1,128)} %seps.1, bf16[1,1024,1024]{2,1,0:T(8,128)(2,1)} %e_hbm.1, bf16[1,3,1024,1024]{3,2,1,0:T(8,128)(2,1)} %p_hbm.1), custom_call_target="tpu_custom_call" | custom-call | flops 19327352832 | bytes 8388608 | tf_op jit(solution)/shard_map/correlators/pallas_call | solution.py:207
  71.7 1.1 %copy.7 = f32[1,3]{1,0:T(1,128)} copy(f32[1,3]{1,0:T(1,128)} %get-tuple-element.4) | data formatting | bytes 24
  72.9 1.1 %copy.8 = f32[1,3]{1,0:T(1,128)} copy(f32[1,3]{1,0:T(1,128)} %get-tuple-element.5) | data formatting | bytes 24

commit v2 on v1

--- a/solution.py
+++ b/solution.py
@@ -10,7 +10,6 @@
 NEV = 256
 H = 2
 CHUNKS = 16
-WINDOW = 3
 BLOCK = 256
 NT = (((1,), (1,)), ((), ()))
 MESH = pl.DeviceIdType.MESH
@@ -79,8 +78,11 @@
         device_id_type=MESH,
     )
 
-    for j in range(WINDOW):
+    def launch(j, carry):
         across_copy(j).start()
+        return carry
+
+    lax.fori_loop(0, CHUNKS, launch, 0)
     mate_copy.start()
 
     acc[...] = jnp.zeros_like(acc)
@@ -93,9 +95,6 @@
         return carry
 
     lax.fori_loop(0, width // 128, flip, 0)
-    for copy in p_copies:
-        copy.wait()
-
     def work(s):
         k = s % count
         first = pl.multiple_of((s // count) * block, block)
@@ -109,8 +108,7 @@
         out = lax.dot_general(both, p_v[k], NT, preferred_element_type=jnp.float32)
         z[k, at, :] = out[:block] + out[block:]
 
-    far = 2 * jnp.int32(1)
-    offsets = (far - 2 * far * row, 2 * far * row - far, 1 - 2 * core, 2 * core - 1)
+    offsets = (H - 2 * H * row, 2 * H * row - H, 1 - 2 * core, 2 * core - 1)
 
     def contract(slot, j):
         def part(i, totals):
@@ -127,49 +125,58 @@
         for k in range(count):
             acc[k] += jnp.where(seps[0, k] == offsets[slot], totals[k], 0.0)
 
-    def step(j, carry):
-        @pl.when(j < steps)
-        def _():
-            work(j)
-
+    def forward(j):
         across_copy(j).wait_recv()
         onward_copy(j).start()
-        across_copy(j).wait_send()
-
-        @pl.when(j + WINDOW < CHUNKS)
-        def _():
-            across_copy(j + WINDOW).start()
-
-        @pl.when(j >= 1)
-        def _():
-            onward_copy(j - 1).wait_recv()
-            share_copy(j - 1).start()
-
-        @pl.when(j == 2)
+
+    def share(j):
+        onward_copy(j).wait_recv()
+        share_copy(j).start()
+
+    def finish(j):
+        share_copy(j).wait_recv()
+        for slot in range(4):
+            contract(slot, j)
+
+    def step(j, carry):
+        forward(j)
+
+        @pl.when(j >= 2)
+        def _():
+            share(j - 2)
+
+        @pl.when(j == 0)
+        def _():
+            for copy in p_copies:
+                copy.wait()
+
+        @pl.when(j < steps)
+        def _():
+            work(j)
+
+        @pl.when(j == 3)
         def _():
             mate_copy.wait_recv()
 
-        @pl.when(j >= 2)
-        def _():
-            contract(0, j - 2)
-            contract(1, j - 2)
-            contract(2, j - 2)
-            share_copy(j - 2).wait_recv()
-            contract(3, j - 2)
+        @pl.when(j >= 3)
+        def _():
+            finish(j - 3)
 
         return carry
 
     lax.fori_loop(0, CHUNKS, step, 0)
     last = CHUNKS - 1
-    for slot in range(3):
-        contract(slot, last - 1)
+    share(last - 1)
+    finish(last - 2)
+    contract(0, last - 1)
+    contract(1, last - 1)
+    contract(2, last - 1)
     contract(0, last)
     contract(2, last)
+    share(last)
+    contract(1, last)
     share_copy(last - 1).wait_recv()
     contract(3, last - 1)
-    onward_copy(last).wait_recv()
-    share_copy(last).start()
-    contract(1, last)
     share_copy(last).wait_recv()
     contract(3, last)
 
@@ -189,6 +196,7 @@
     pass_on.start()
 
     def drain(j, carry):
+        across_copy(j).wait_send()
         onward_copy(j).wait_send()
         share_copy(j).wait_send()
         return carry

time: 74.2 us -> 64.4 us (0.87)
  Pallas kernels: 71.1 us -> 61.3 us
    pallas_call x1, Pallas kernels: 71.1 us -> 61.3 us  [body(): pl.pallas_call(functools.partial(kernel, peers), out_shape=(small, small)...]
where the time goes in v2:
time: 64.4 us; the launch traced here: 64.2 us
  Pallas kernels  61.3 us (95%)
  local copies, waits for them, and re-layouts  2.25 us (3%)
    pallas_call x1, Pallas kernels, body(): pl.pallas_call(functools.partial(kernel, peers), out_shape=(small, small)...  61.3 us
    unnamed x2, local copies, waits for them, and re-layouts  2.25 us

profile of v2, /device:TPU:0, one launch (start us, length us, event | category | flops | bytes accessed | tf_op | source)
XLA Modules:
  0.0 64.2 jit_solution(16123916135439870108)
XLA Ops:
  0.6 61.3 %correlators.1 = (f32[1,3]{1,0:T(1,128)}, f32[1,3]{1,0:T(1,128)}) custom-call(s32[1,3]{1,0:T(1,128)} %seps.1, bf16[1,1024,1024]{2,1,0:T(8,128)(2,1)} %e_hbm.1, bf16[1,3,1024,1024]{3,2,1,0:T(8,128)(2,1)} %p_hbm.1), custom_call_target="tpu_custom_call" | custom-call | flops 19327352832 | bytes 8388608 | tf_op jit(solution)/shard_map/correlators/pallas_call | solution.py:215
  62.0 1.1 %copy.7 = f32[1,3]{1,0:T(1,128)} copy(f32[1,3]{1,0:T(1,128)} %get-tuple-element.4) | data formatting | bytes 24
  63.1 1.1 %copy.8 = f32[1,3]{1,0:T(1,128)} copy(f32[1,3]{1,0:T(1,128)} %get-tuple-element.5) | data formatting | bytes 24

commit v3 on v2

--- a/solution.py
+++ b/solution.py
@@ -16,7 +16,7 @@
 
 
 def kernel(
-    peers, seps, e_hbm, p_hbm, corr_ref, pair_ref,
+    peers, seps, e_hbm, p_hbm, out_ref,
     es, p_v, z, buf, acc, mine, near, local_sem, send, recv, small_sem,
 ):
     count, width = p_v.shape[0], p_v.shape[1]
@@ -39,12 +39,9 @@
         pl.semaphore_signal(barrier, inc=1, device_id={"tm": peer}, device_id_type=MESH)
 
     e_copy = pltpu.make_async_copy(e_hbm.at[0], es, local_sem.at[0])
-    e_copy.start()
     p_copies = [
         pltpu.make_async_copy(p_hbm.at[0, k], p_v.at[k], local_sem.at[1 + k]) for k in range(count)
     ]
-    for copy in p_copies:
-        copy.start()
     pl.semaphore_wait(barrier, 4)
 
     def rows_of(j):
@@ -78,14 +75,22 @@
         device_id_type=MESH,
     )
 
+    def forward(j):
+        across_copy(j).wait_recv()
+        onward_copy(j).start()
+
     def launch(j, carry):
         across_copy(j).start()
         return carry
 
     lax.fori_loop(0, CHUNKS, launch, 0)
     mate_copy.start()
+    e_copy.start()
+    for copy in p_copies:
+        copy.start()
 
     acc[...] = jnp.zeros_like(acc)
+    forward(0)
     e_copy.wait()
     sign_row = jnp.where(lax.broadcasted_iota(jnp.int32, (1, width), 1) // NEV < 2, 1.0, -1.0)
 
@@ -125,10 +130,6 @@
         for k in range(count):
             acc[k] += jnp.where(seps[0, k] == offsets[slot], totals[k], 0.0)
 
-    def forward(j):
-        across_copy(j).wait_recv()
-        onward_copy(j).start()
-
     def share(j):
         onward_copy(j).wait_recv()
         share_copy(j).start()
@@ -139,7 +140,9 @@
             contract(slot, j)
 
     def step(j, carry):
-        forward(j)
+        @pl.when(j >= 1)
+        def _():
+            forward(j)
 
         @pl.when(j >= 2)
         def _():
@@ -203,24 +206,23 @@
 
     lax.fori_loop(0, CHUNKS, drain, 0)
     mate_copy.wait_send()
-    corr_ref[...] = values[:1, :count]
+    out_ref[0:1, :] = values[:1, :count]
     pass_on.wait()
-    pair_ref[...] = values[:1, :count] * near[:1, :count]
+    out_ref[1:2, :] = values[:1, :count] * near[:1, :count]
 
 
 def body(elemental, peramb, seps):
     peers = lax.axis_size("tm")
     count, width = peramb.shape[1], peramb.shape[2]
-    small = jax.ShapeDtypeStruct((1, count), jnp.float32)
-    return pl.pallas_call(
+    out = pl.pallas_call(
         functools.partial(kernel, peers),
-        out_shape=(small, small),
+        out_shape=jax.ShapeDtypeStruct((2, count), jnp.float32),
         in_specs=[
             pl.BlockSpec(memory_space=pltpu.SMEM),
             pl.BlockSpec(memory_space=pl.ANY),
             pl.BlockSpec(memory_space=pl.ANY),
         ],
-        out_specs=(pl.BlockSpec(memory_space=pltpu.VMEM),) * 2,
+        out_specs=pl.BlockSpec(memory_space=pltpu.VMEM),
         scratch_shapes=[
             pltpu.VMEM((width, width), jnp.bfloat16),
             pltpu.VMEM((count, width, width), jnp.bfloat16),
@@ -242,6 +244,7 @@
         ),
         name="correlators",
     )(seps, elemental, peramb)
+    return out[:1], out[1:]
 
 
 def solution(mesh):

time: 64.4 us -> 63.4 us (0.984)
  local copies, waits for them, and re-layouts: 2.25 us -> 1.25 us
    unnamed x2 -> x0, local copies, waits for them, and re-layouts: 2.25 us -> none
    slice x0 -> x1, local copies, waits for them, and re-layouts: none -> 1.25 us  [body(): return (out[:1], out[1:])]
where the time goes in v3:
time: 63.4 us; the launch traced here: 63.2 us
  Pallas kernels  61.4 us (97%)
  local copies, waits for them, and re-layouts  1.25 us (2%)
  between operations  0.64 us (1%)
    pallas_call x1, Pallas kernels, body(): pl.pallas_call(functools.partial(kernel, peers), out_shape=jax.ShapeDtype...  61.4 us

profile of v3, /device:TPU:0, one launch (start us, length us, event | category | flops | bytes accessed | tf_op | source)
XLA Modules:
  0.0 63.2 jit_solution(11321215829775742814)
XLA Ops:
  0.6 61.4 %correlators.1 = f32[2,3]{1,0:T(2,128)} custom-call(s32[1,3]{1,0:T(1,128)} %seps.1, bf16[1,1024,1024]{2,1,0:T(8,128)(2,1)} %e_hbm.1, bf16[1,3,1024,1024]{3,2,1,0:T(8,128)(2,1)} %p_hbm.1), custom_call_target="tpu_custom_call" | custom-call | flops 19327352832 | bytes 8388608 | tf_op jit(solution)/shard_map/correlators/pallas_call | solution.py:217
  62.0 1.3 %fusion = (f32[1,3]{1,0:T(1,128)}, f32[1,3]{1,0:T(1,128)}) fusion(f32[2,3]{1,0:T(2,128)} %correlators.1), kind=kLoop, calls=%fused_computation | loop fusion | bytes 48 | tf_op jit(solution)/shard_map/slice | solution.py:247

commit v4 on v3

--- a/solution.py
+++ b/solution.py
@@ -84,13 +84,13 @@
         return carry
 
     lax.fori_loop(0, CHUNKS, launch, 0)
-    mate_copy.start()
     e_copy.start()
     for copy in p_copies:
         copy.start()
 
     acc[...] = jnp.zeros_like(acc)
     forward(0)
+    mate_copy.start()
     e_copy.wait()
     sign_row = jnp.where(lax.broadcasted_iota(jnp.int32, (1, width), 1) // NEV < 2, 1.0, -1.0)
 
@@ -186,7 +186,7 @@
     lane = lax.broadcasted_iota(jnp.int32, (8, 128), 1)
     values = jnp.zeros((8, 128), jnp.float32)
     for k in range(count):
-        values = jnp.where(lane == k, jnp.sum(acc[k]), values)
+        values = jnp.where(lane == k, jnp.sum(acc[k], axis=(0, 1), keepdims=True), values)
     mine[...] = values
     pass_on = pltpu.make_async_remote_copy(
         src_ref=mine,

time: 63.4 us -> 63.4 us (level)
  no operation moved by 1% of the time
where the time goes in v4:
time: 63.4 us; the launch traced here: 63.2 us
  Pallas kernels  61.4 us (97%)
  local copies, waits for them, and re-layouts  1.25 us (2%)
  between operations  0.64 us (1%)
    pallas_call x1, Pallas kernels, body(): pl.pallas_call(functools.partial(kernel, peers), out_shape=jax.ShapeDtype...  61.4 us

profile of v4, /device:TPU:0, one launch (start us, length us, event | category | flops | bytes accessed | tf_op | source)
XLA Modules:
  0.0 63.2 jit_solution(6466696762001743433)
XLA Ops:
  0.6 61.4 %correlators.1 = f32[2,3]{1,0:T(2,128)} custom-call(s32[1,3]{1,0:T(1,128)} %seps.1, bf16[1,1024,1024]{2,1,0:T(8,128)(2,1)} %e_hbm.1, bf16[1,3,1024,1024]{3,2,1,0:T(8,128)(2,1)} %p_hbm.1), custom_call_target="tpu_custom_call" | custom-call | flops 19327352832 | bytes 8388608 | tf_op jit(solution)/shard_map/correlators/pallas_call | solution.py:217
  62.0 1.3 %fusion = (f32[1,3]{1,0:T(1,128)}, f32[1,3]{1,0:T(1,128)}) fusion(f32[2,3]{1,0:T(2,128)} %correlators.1), kind=kLoop, calls=%fused_computation | loop fusion | bytes 48 | tf_op jit(solution)/shard_map/slice | solution.py:247
